TPU v7x, 256 devices: a whole 4x4x8 slice. The times are simulated.
256 devices in a mesh: section: 32 (over z_hi, y, core), dp: 8 (over z_lo, x).
Axes of the slice: x: 4, y: 4, z: 8 (z_hi: 4, z_lo: 2; z = z_hi * 2 + z_lo), core: 2. Of those that a mesh axis runs over, the one named last changes fastest.
Arguments:
- activations: bfloat16 [32, 64, 64, 4096], P('section', 'dp'), may hold values from -6 to 6
- out_grads: bfloat16 [32, 64, 64, 4096], P('section', 'dp'), may hold values from -6 to 6
- proj_in: bfloat16 [32, 2, 4096, 128], P('section'), may hold values from -0.09375 to 0.09375
- proj_out: bfloat16 [32, 2, 64, 4096], P('section'), may hold values from -0.09375 to 0.09375
- earlier_gram: float32 [8192, 8192], P('section', 'dp'), may hold values from -4 to 4, as said below
Outputs:
- gram: float32 [8192, 8192], P('section', 'dp')
Inputs may be any that keep to these rules, and one draw needn't show every extreme that they name: earlier_gram is symmetric.
All inputs are finite; a program needn't handle non-finite values.
Results may differ from a plain program's by a relative error of at most 0.0013.
Values sent between devices are 32-bit elements; how exact they have to be, the bound alone decides.
No kernel may reach another device: no remote copies, remote signals or barrier semaphores. Data moves between devices by JAX's collectives and lax.ppermute only.
A program may use at most 64 MiB of HBM per device.

v0:
```python
import math
import jax
import jax.numpy as jnp
from jax import lax
from jax.sharding import PartitionSpec as P

PROJ = 2
LEN = 64


def per_device(activations, out_grads, proj_in, proj_out, earlier_gram):
    layer_act = activations[0]
    layer_grad = out_grads[0]
    layer_in = proj_in[0]
    layer_out = proj_out[0]
    low_in = jnp.einsum(
        "etd,pdm->petm", layer_act, layer_in, preferred_element_type=jnp.float32
    ).astype(jnp.bfloat16)
    low_out = jnp.einsum(
        "pkd,etd->pekt", layer_out, layer_grad, preferred_element_type=jnp.float32
    ).astype(jnp.bfloat16)
    partial_terms = jnp.einsum(
        "pekt,petm->ekm", low_out, low_in, preferred_element_type=jnp.float32
    )
    local_count = partial_terms.shape[0]
    partial_terms = partial_terms.reshape(local_count, -1)
    n_layers = lax.axis_size("section")
    n_groups = lax.axis_size("dp")
    total_examples = local_count * n_groups
    scale = 1.0 / math.sqrt(LEN * n_layers * PROJ)
    row_width = earlier_gram.shape[0]
    col_width = earlier_gram.shape[1]
    row_start = lax.axis_index("section") * row_width
    col_start = lax.axis_index("dp") * col_width
    placed = jnp.zeros((total_examples, partial_terms.shape[1]), jnp.float32)
    placed = lax.dynamic_update_slice_in_dim(
        placed, partial_terms, lax.axis_index("dp") * local_count, 0
    )
    features = lax.psum(placed, ("section", "dp")) * scale
    row_block = lax.dynamic_slice_in_dim(features, row_start, row_width, 1)
    col_block = lax.dynamic_slice_in_dim(features, col_start, col_width, 1)
    outer = jnp.dot(row_block.T, col_block, precision=lax.Precision.HIGHEST)
    return earlier_gram + outer / total_examples


def solution(mesh):
    return jax.shard_map(
        per_device,
        mesh=mesh,
        in_specs=(
            P("section", "dp", None, None),
            P("section", "dp", None, None),
            P("section", None, None, None),
            P("section", None, None, None),
            P("section", "dp"),
        ),
        out_specs=P("section", "dp"),
        check_vma=False,
    )
```

profile of v0, /device:TPU:2, one launch (start us, length us, event | category | flops | bytes accessed | tf_op | source)
XLA Modules:
  0.0 292.4 jit_solution(597952820103288470)
XLA Ops:
  6.5 0.0 copy-start
  6.5 0.0 all-reduce.2.cloned.1.call-start
  6.5 4.8 %fusion.14 = bf16[2,8,64,64]{3,2,0,1:T(8,128)(2,1)S(1)} fusion(bf16[1,8,64,4096]{3,2,1,0:T(8,128)(2,1)} %param.6, bf16[1,2,64,4096]{3,2,1,0:T(8,128)(2,1)} %param.8), kind=kOutput, calls=%fused_computation.9 | convolution fusion | flops 536936448 | bytes 5373952 | tf_op jit(solution)/shard_map/pkd,etd->pekt/dot_general | solution.py:19
  11.3 0.0 copy-done
  11.3 3.6 %convolution_bitcast_fusion = f32[1,8,64,128]{3,2,1,0:T(8,128)S(1)} fusion(bf16[2,8,64,64]{3,2,0,1:T(8,128)(2,1)S(1)} %fusion.14, bf16[1,8,64,4096]{3,2,1,0:T(8,128)(2,1)} %param.5, bf16[1,2,4096,128]{3,2,1,0:T(8,128)(2,1)S(1)} %copy-done), kind=kOutput, calls=%fused_computation.10 | convolution fusion | flops 1090650112 | bytes 6684672 | tf_op jit(solution)/shard_map/pekt,petm->ekm/dot_general | solution.py:22
  15.0 1.5 broadcast_in_dim.3
  16.5 0.9 bitcast_dynamic-update-slice_fusion
  17.3 0.0 all-reduce.2.cloned.1.call-update
  17.4 0.0 copy-start.1
  17.4 264.4 %all-reduce.2.cloned.1.call-done = f32[64,8192]{1,0:T(8,128)} async-done(((f32[64,8192]{1,0:T(8,128)}), f32[64,8192]{1,0:T(8,128)}) %all-reduce.2.cloned.1.call-update) | async-done | bytes 2097168 | tf_op jit(solution)/shard_map/psum | solution.py:39
  281.8 1.8 broadcast_multiply_fusion
  283.5 0.0 copy-done.1
  283.5 2.0 fusion.5
Async XLA Ops:
  6.5 4.8 %copy-start = (bf16[1,2,4096,128]{3,2,1,0:T(8,128)(2,1)S(1)}, bf16[1,2,4096,128]{3,2,1,0:T(8,128)(2,1)}, u32[]{:S(2)}) copy-start(bf16[1,2,4096,128]{3,2,1,0:T(8,128)(2,1)} %param.7) | copy-start | bytes 6291460
  6.5 275.2 %all-reduce.2.cloned.1.call-start = ((), (), s32[]{:S(2)}) async-start(), calls=%async_computation | async-start | bytes 4194304 | tf_op jit(solution)/shard_map/psum | solution.py:39
  17.4 266.2 %copy-start.1 = (f32[256,1024]{1,0:T(8,128)S(1)}, f32[256,1024]{1,0:T(8,128)}, u32[]{:S(2)}) copy-start(f32[256,1024]{1,0:T(8,128)} %param.9) | copy-start | bytes 3145732
Sparse Core Ops, SparseCore 0:
  17.5 264.2 all-reduce.1
where the time goes:
time: 293 us; the launch traced here: 292 us
  waiting for transfers between devices  264 us (90%)
  between operations  13.4 us (5%)
  matrix products  10.4 us (4%)
    psum x1, waiting for transfers between devices, per_device(): features = lax.psum(placed, ('section', 'dp')) * scale  264 us
  transfers between devices with their start and end apart: 1, of which 1 were waited for; matrix products, arithmetic and copies ran while one was open for 0% of the time, Pallas kernels for 0%

commit v1 on v0

--- a/solution.py
+++ b/solution.py
@@ -9,6 +9,11 @@
 
 
 def per_device(activations, out_grads, proj_in, proj_out, earlier_gram):
+
+    def block_report(load):
+        local_now = jax.lax.psum(load, "dp")
+        return jax.lax.psum(local_now, "section")
+
     layer_act = activations[0]
     layer_grad = out_grads[0]
     layer_in = proj_in[0]
@@ -36,7 +41,7 @@
     placed = lax.dynamic_update_slice_in_dim(
         placed, partial_terms, lax.axis_index("dp") * local_count, 0
     )
-    features = lax.psum(placed, ("section", "dp")) * scale
+    features = block_report(placed) * scale
     row_block = lax.dynamic_slice_in_dim(features, row_start, row_width, 1)
     col_block = lax.dynamic_slice_in_dim(features, col_start, col_width, 1)
     outer = jnp.dot(row_block.T, col_block, precision=lax.Precision.HIGHEST)

time: 293 us -> 414 us (1.41)
  waiting for transfers between devices: 264 us -> 385 us
    psum x1 -> x2, waiting for transfers between devices: 264 us -> 385 us  [the longest x1 295 us: block_report(): return jax.lax.psum(local_now, 'section')]
  transfers between devices with their start and end apart: 1 -> 2, of which waited for: 1 -> 2; matrix products, arithmetic and copies ran while one was open for 0% -> 0% of each run, Pallas kernels for 0% -> 0%
where the time goes in v1:
time: 414 us; the launch traced here: 413 us
  waiting for transfers between devices  385 us (93%)
  between operations  13.4 us (3%)
  matrix products  10.4 us (3%)
    psum x1, waiting for transfers between devices, block_report(): return jax.lax.psum(local_now, 'section')  295 us
    psum x1, waiting for transfers between devices, block_report(): local_now = jax.lax.psum(load, 'dp')  89.8 us
  transfers between devices with their start and end apart: 2, of which 2 were waited for; matrix products, arithmetic and copies ran while one was open for 0% of the time, Pallas kernels for 0%

profile of v1, /device:TPU:2, one launch (start us, length us, event | category | flops | bytes accessed | tf_op | source)
XLA Modules:
  0.0 413.2 jit_solution(18237705975545066314)
XLA Ops:
  6.5 0.0 copy-start
  6.5 0.0 all-reduce.3.cloned.1.call-start
  6.5 4.8 %fusion.14 = bf16[2,8,64,64]{3,2,0,1:T(8,128)(2,1)S(1)} fusion(bf16[1,8,64,4096]{3,2,1,0:T(8,128)(2,1)} %param.6, bf16[1,2,64,4096]{3,2,1,0:T(8,128)(2,1)} %param.8), kind=kOutput, calls=%fused_computation.9 | convolution fusion | flops 536936448 | bytes 5373952 | tf_op jit(solution)/shard_map/pkd,etd->pekt/dot_general | solution.py:24
  11.3 0.0 copy-done
  11.3 3.6 convolution_bitcast_fusion
  15.0 1.5 broadcast_in_dim.3
  16.5 0.9 bitcast_dynamic-update-slice_fusion
  17.3 0.0 all-reduce.3.cloned.1.call-update
  17.3 0.0 all-reduce.5.cloned.1.call-start
  17.4 89.8 %all-reduce.3.cloned.1.call-done = f32[64,8192]{1,0:T(8,128)} async-done(((f32[64,8192]{1,0:T(8,128)}), f32[64,8192]{1,0:T(8,128)}) %all-reduce.3.cloned.1.call-update) | async-done | bytes 2097168 | tf_op jit(solution)/shard_map/psum | solution.py:14
  107.2 0.0 all-reduce.5.cloned.1.call-update
  107.2 0.0 copy-start.1
  107.3 295.3 %all-reduce.5.cloned.1.call-done = f32[64,8192]{1,0:T(8,128)} async-done(((f32[64,8192]{1,0:T(8,128)}), f32[64,8192]{1,0:T(8,128)}) %all-reduce.5.cloned.1.call-update) | async-done | bytes 2097168 | tf_op jit(solution)/shard_map/psum | solution.py:15
  402.6 1.8 broadcast_multiply_fusion
  404.4 0.0 copy-done.1
  404.4 2.0 fusion.5
Async XLA Ops:
  6.5 4.8 %copy-start = (bf16[1,2,4096,128]{3,2,1,0:T(8,128)(2,1)S(1)}, bf16[1,2,4096,128]{3,2,1,0:T(8,128)(2,1)}, u32[]{:S(2)}) copy-start(bf16[1,2,4096,128]{3,2,1,0:T(8,128)(2,1)} %param.7) | copy-start | bytes 6291460
  6.5 100.7 %all-reduce.3.cloned.1.call-start = ((), (), s32[]{:S(2)}) async-start(), calls=%async_computation | async-start | bytes 4194304 | tf_op jit(solution)/shard_map/psum | solution.py:14
  17.3 385.3 %all-reduce.5.cloned.1.call-start = ((), (), s32[]{:S(2)}) async-start(), calls=%async_computation.1 | async-start | bytes 4194304 | tf_op jit(solution)/shard_map/psum | solution.py:15
  107.2 297.1 %copy-start.1 = (f32[256,1024]{1,0:T(8,128)S(1)}, f32[256,1024]{1,0:T(8,128)}, u32[]{:S(2)}) copy-start(f32[256,1024]{1,0:T(8,128)} %param.9) | copy-start | bytes 3145732
Sparse Core Ops, SparseCore 0:
  17.5 89.7 all-reduce.2
  109.8 292.7 all-reduce.4
